TPU v7x, 32 devices: a whole 2x2x4 slice. The times are simulated.
32 devices in a mesh: groups: 2 (over y), band: 8 (over z, x), blk: 2 (over core).
Axes of the slice: x: 2, y: 2, z: 4, core: 2. Of those that a mesh axis runs over, the one named last changes fastest.
Arguments:
- valence: bfloat16 [256, 4096], P(('groups', 'band')), parts along dimension 0, may hold values from -6 to 6
- conduction: bfloat16 [4096, 128], P('band', ('groups', 'blk')), parts along dimension 1, may hold values from -6 to 6
- val_energy: float32 [256], P(('groups', 'band')), parts along dimension 0, may hold values from -12 to -1
- cond_energy: float32 [128], P(('groups', 'blk')), parts along dimension 0, may hold values from 0.5 to 10
- gvectors: int32 [3, 1024], P(None, 'groups'), parts along dimension 1, may hold values from -8 to 7
Outputs:
- chi: float32 [2, 1024, 512], P(None, ('groups', 'band'), 'blk'), parts along dimension 1
There are 2 independent parts, one for each index of `groups`. A program takes and returns all parts, laid end to end along the dimension named above; each array names one. Nothing has to cross between parts.
All inputs are finite; a program needn't handle non-finite values.
Results may differ from a plain program's by a relative error of at most 0.0037.
Values may be sent and summed in bfloat16 or wider, within the bound.
A program may use at most 64 MiB of HBM per device.

v0:
```python
import math

import jax
import jax.numpy as jnp
from jax import lax
from jax.sharding import PartitionSpec as P

GRID = 16


def table_rows(gvectors, grid, start, count):
    total_points = grid * grid * grid
    points = start + jnp.arange(count, dtype=jnp.int32)
    xs = points // (grid * grid)
    ys = points // grid % grid
    zs = points % grid
    phase_int = (
        xs[:, None] * gvectors[0][None, :]
        + ys[:, None] * gvectors[1][None, :]
        + zs[:, None] * gvectors[2][None, :]
    )
    phase_int = jnp.mod(phase_int, grid)
    phase = phase_int.astype(jnp.float32) * (2.0 * math.pi / grid)
    scale = 1.0 / math.sqrt(total_points)
    return jnp.concatenate([jnp.cos(phase) * scale, -jnp.sin(phase) * scale], axis=1).astype(
        jnp.bfloat16
    )


def chi_part(weighted, elements, width, row_start, row_count, col_start, col_count):
    dims = (((0,), (0,)), ((), ()))
    left_re = lax.dynamic_slice_in_dim(weighted, row_start, row_count, 1)
    left_im = lax.dynamic_slice_in_dim(weighted, row_start + width, row_count, 1)
    right_re = lax.dynamic_slice_in_dim(elements, col_start, col_count, 1)
    right_im = lax.dynamic_slice_in_dim(elements, col_start + width, col_count, 1)
    real_part = lax.dot_general(
        left_re, right_re, dims, preferred_element_type=jnp.float32
    ) + lax.dot_general(left_im, right_im, dims, preferred_element_type=jnp.float32)
    imag_part = lax.dot_general(
        left_im, right_re, dims, preferred_element_type=jnp.float32
    ) - lax.dot_general(left_re, right_im, dims, preferred_element_type=jnp.float32)
    return (real_part, imag_part)


def per_device(valence, conduction, val_energy, cond_energy, gvectors):
    width = gvectors.shape[1]
    val_count = valence.shape[0]
    cond_count = conduction.shape[1]
    n_band = lax.axis_size("band")
    n_blk = lax.axis_size("blk")
    row_block = width // n_band
    col_block = width // n_blk
    points_all = valence.shape[1]
    point_block = min(512, points_all)
    gathered = lax.all_gather(conduction, "band", axis=0, tiled=True)
    cond_rows = jnp.transpose(gathered).astype(jnp.float32)
    summed = jnp.zeros((val_count * cond_count, 2 * width), jnp.float32)
    for block_index in range(points_all // point_block):
        start = block_index * point_block
        vals = valence[:, start : start + point_block].astype(jnp.float32)
        conds = cond_rows[:, start : start + point_block]
        pair = (vals[:, None, :] * conds[None, :, :]).astype(jnp.bfloat16).reshape(-1, point_block)
        tab_block = table_rows(gvectors, GRID, start, point_block)
        summed = summed + jnp.dot(pair, tab_block, preferred_element_type=jnp.float32)
    elements = summed.astype(jnp.bfloat16)
    val_total = val_count * n_band
    cond_total = cond_count * n_blk
    norm = 1.0 / math.sqrt(val_total * cond_total)
    factor = (-1.0 / (cond_energy[None, :] - val_energy[:, None]) * norm).reshape(-1, 1)
    weighted = (elements.astype(jnp.float32) * factor).astype(jnp.bfloat16)
    band_index = lax.axis_index("band")
    blk_index = lax.axis_index("blk")
    real_part, imag_part = chi_part(weighted, elements, width, 0, width, 0, width)
    total = lax.psum(jnp.stack([real_part, imag_part]), ("band", "blk"))
    mine = lax.dynamic_slice_in_dim(total, band_index * row_block, row_block, 1)
    return lax.dynamic_slice_in_dim(mine, blk_index * col_block, col_block, 2)


def solution(mesh):
    in_specs = (
        P(("groups", "band"), None),
        P("band", ("groups", "blk")),
        P(("groups", "band")),
        P(("groups", "blk")),
        P(None, "groups"),
    )
    out_specs = P(None, ("groups", "band"), "blk")
    return jax.shard_map(
        per_device, mesh=mesh, in_specs=in_specs, out_specs=out_specs, check_vma=False
    )
```

profile of v0, /device:TPU:1, one launch (start us, length us, event | category | flops | bytes accessed | tf_op | source)
XLA Modules:
  0.0 193.7 jit_solution(3021185840704829738)
XLA Ops:
  6.5 0.0 copy-start
  6.5 0.0 copy-start.1
  6.5 0.0 copy-start.2
  6.5 0.0 all-reduce.2.cloned.1.call-start
  6.7 0.8 fusion.118
  7.5 26.1 %all_gather.3 = bf16[4096,32]{0,1:T(8,128)(2,1)S(1)} all-gather(bf16[512,32]{0,1:T(8,128)(2,1)} %param.6), channel_id=1, replica_groups=mesh['groups'=2,'band'=8,'blk'=2] {'band'}, dimensions={0}, use_global_device_ids=true | all-gather | bytes 294912 | tf_op jit(solution)/shard_map/all_gather | solution.py:55
  33.7 0.0 copy-done
  33.7 0.0 copy-done.1
  33.7 0.0 copy-done.2
  33.7 0.1 divide_multiply_fusion
  33.8 0.1 mul.599
  33.9 0.3 multiply_convert_fusion.21
  34.2 22.7 %multiply_convert_fusion.2 = (bf16[512,512]{1,0:T(8,128)(2,1)S(1)}, bf16[512,512]{1,0:T(8,128)(2,1)S(1)}, bf16[512,512]{1,0:T(8,128)(2,1)S(1)}, bf16[512,512]{1,...) fusion(s32[512]{0:T(512)S(1)} %bitcast.35, ...), kind=kLoop, calls=%fused_computation.87 | loop fusion | flops 30146560 | bytes 5279744 | tf_op jit(solution)/shard_map/convert.1
  56.9 0.7 fusion.30
  57.6 0.2 multiply_convert_fusion.15
  57.9 0.7 fusion.34
  58.6 0.7 fusion.38
  59.3 0.2 multiply_convert_fusion.9
  59.6 0.7 fusion.42
  60.3 14.0 %multiply_convert_fusion.23 = (bf16[512,512]{1,0:T(8,128)(2,1)S(1)}, bf16[512,512]{1,0:T(8,128)(2,1)S(1)}, bf16[512,512]{1,0:T(8,128)(2,1)S(1)}, bf16[512,512]{1...) fusion(s32[512]{0:T(512)S(1)} %bitcast.36, s32[512]{0:T(512)S(1)} %get-tuple-element.82, ...), kind=kLoop, calls=%fused_computation.108 | loop fusion | flops 18087936 | bytes 3170304 | tf_op jit(solution)/shard_map/convert.15
  74.3 0.7 fusion.26
  75.0 0.7 fusion.46
  75.7 0.2 multiply_convert_fusion.3
  75.9 0.7 fusion.50
  76.6 1.2 multiply_convert_fusion
  77.8 0.5 fusion.63
  78.2 0.5 fusion.59
  78.7 0.5 fusion.1
  79.2 0.5 fusion
  79.7 1.5 pad_maximum_fusion
  81.1 0.0 all-reduce.2.cloned.1.call-update
  81.2 104.0 %all-reduce.2.cloned.1.call-done = f32[2,512,512]{2,1,0:T(8,128)} async-done(((f32[2,512,512]{2,1,0:T(8,128)}), f32[2,512,512]{2,1,0:T(8,128)}) %all-reduce.2.cloned.1.call-update) | async-done | bytes 2097168 | tf_op jit(solution)/shard_map/psum | solution.py:74
  185.2 1.7 constant_dynamic-slice_fusion
  (16 shorter events, 0.2 us)
Async XLA Ops:
  6.5 27.2 %copy-start = (bf16[16,4096]{1,0:T(8,128)(2,1)S(1)}, bf16[16,4096]{1,0:T(8,128)(2,1)}, u32[]{:S(2)}) copy-start(bf16[16,4096]{1,0:T(8,128)(2,1)} %param.5) | copy-start | bytes 393220
  6.5 27.2 %copy-start.1 = (f32[16]{0:T(128)S(1)}, f32[16]{0:T(128)}, u32[]{:S(2)}) copy-start(f32[16]{0:T(128)} %param.7) | copy-start | bytes 196
  6.5 27.2 %copy-start.2 = (f32[32]{0:T(128)S(1)}, f32[32]{0:T(128)}, u32[]{:S(2)}) copy-start(f32[32]{0:T(128)} %param.8) | copy-start | bytes 388
  6.5 178.7 %all-reduce.2.cloned.1.call-start = ((), (), s32[]{:S(2)}) async-start(), calls=%async_computation | async-start | bytes 4194304 | tf_op jit(solution)/shard_map/psum | solution.py:74
Sparse Core Ops, SparseCore 0:
  81.3 103.8 all-reduce.1
where the time goes:
time: 195 us; the launch traced here: 194 us
  waiting for transfers between devices  104 us (53%)
  other arithmetic  39.4 us (20%)
  blocking collectives  26.1 us (13%)
  between operations  13.6 us (7%)
  matrix products  7.99 us (4%)
  local copies, waits for them, and re-layouts  2.62 us (1%)
    psum x1, waiting for transfers between devices, per_device(): total = lax.psum(jnp.stack([real_part, imag_part]), ('band', 'blk'))  104 us
    another operation x2, other arithmetic  36.7 us
    all_gather x1, blocking collectives, per_device(): gathered = lax.all_gather(conduction, 'band', axis=0, tiled=True)  26.1 us
    dot_general x8, matrix products, per_device(): jnp.dot(pair, tab_block, preferred_element_type=jnp.float32)  6.11 us
  transfers between devices with their start and end apart: 1, of which 1 were waited for; matrix products, arithmetic and copies ran while one was open for 0% of the time, Pallas kernels for 0%

commit v1 on v0

--- a/solution.py
+++ b/solution.py
@@ -1,11 +1,323 @@
+import functools
 import math
 
 import jax
 import jax.numpy as jnp
 from jax import lax
+from jax.experimental import pallas as pl
+from jax.experimental.pallas import tpu as pltpu
 from jax.sharding import PartitionSpec as P
 
 GRID = 16
+F32 = jnp.float32
+BF16 = jnp.bfloat16
+NT = (((1,), (1,)), ((), ()))
+
+
+def cos_sin(theta):
+    t = theta * theta
+    cos = jnp.full_like(t, 1.0 / math.factorial(16))
+    for n in range(14, -1, -2):
+        cos = cos * t + (-1.0) ** (n // 2) / math.factorial(n)
+    sin = jnp.full_like(t, 1.0 / math.factorial(17))
+    for n in range(15, 0, -2):
+        sin = sin * t + (-1.0) ** (n // 2) / math.factorial(n)
+    return cos, sin * theta
+
+
+def unit(phase):
+    m = phase - GRID * jnp.floor(phase * (1.0 / GRID))
+    cos, sin = cos_sin((m - GRID // 2) * (2.0 * math.pi / GRID))
+    return -cos, sin
+
+
+def chi_kernel(
+    n_band, n_blk, val_ref, cond_ref, ve_ref, ce_ref, gv_ref, out_ref,
+    gpad, gcol, prot, cond_all, table, pair, acc, wgt, dst_,
+    send1, own1, recv1, sendx, recvx, sendz, recvz, sende, recve, other,
+    ag_send, ag_fwd, ag_recv, s1_send, s1_recv, sx_send, sx_recv, sz_send, sz_recv, se_send, se_recv,
+):
+    nz = n_band // 2
+    n_val, total_points = val_ref.shape
+    block_points, n_cond = cond_ref.shape
+    width = gv_ref.shape[1]
+    zpoints = 2 * block_points
+    plane = GRID * GRID
+    xs_per = zpoints // plane
+    row_block = width // n_band
+    col_block = width // n_blk
+    per_blk = col_block // row_block
+
+    b = lax.axis_index("band")
+    k = lax.axis_index("blk")
+    z = b // 2
+    x = b % 2
+    xn = b + 1 - 2 * x
+    kn = 1 - k
+
+    def dev(band, blk):
+        return {"band": band, "blk": blk}
+
+    def zpeer(t):
+        return lax.rem(z + t, nz)
+
+    def copy(src, dst, s, r, band, blk):
+        return pltpu.make_async_remote_copy(
+            src_ref=src, dst_ref=dst, send_sem=s, recv_sem=r,
+            device_id=dev(band, blk), device_id_type=pl.DeviceIdType.MESH,
+        )
+
+    barrier = pltpu.get_barrier_semaphore()
+
+    def greet(band, blk):
+        pl.semaphore_signal(barrier, inc=1, device_id=dev(band, blk), device_id_type=pl.DeviceIdType.MESH)
+
+    greet(b, kn)
+    greet(xn, k)
+    for t in range(1, nz):
+        greet(zpeer(t) * 2 + x, k)
+    mirror_blk = b // per_blk
+    for j in range(per_blk):
+        @pl.when(k * per_blk + j != b)
+        def _():
+            greet(k * per_blk + j, mirror_blk)
+
+    eye = (
+        lax.broadcasted_iota(jnp.int32, (n_cond, n_cond), 0) == lax.broadcasted_iota(jnp.int32, (n_cond, n_cond), 1)
+    ).astype(F32).astype(BF16)
+    cond_all[b] = lax.dot_general(eye, cond_ref[...], NT, preferred_element_type=F32).astype(BF16)
+
+    pl.semaphore_wait(barrier, 1 + nz + per_blk - jnp.where(mirror_blk == k, 1, 0))
+
+    sends = []
+    for t in range(1, nz):
+        c = copy(cond_all.at[b], cond_all.at[b], ag_send.at[t], ag_recv.at[b], zpeer(t) * 2 + x, k)
+        c.start()
+        sends.append(c)
+    c = copy(cond_all.at[b], cond_all.at[b], ag_send.at[0], ag_recv.at[b], xn, k)
+    c.start()
+    sends.append(c)
+
+    gpad[...] = jnp.zeros_like(gpad)
+    gpad[0:3, :] = gv_ref[...].astype(F32)
+    gcol[...] = jnp.transpose(gpad[...])
+    lane = lax.broadcasted_iota(jnp.int32, (1, 128), 1).astype(F32)
+    pc, ps = unit(gcol[:, 0:1] * lane)
+    prot[0] = pc
+    prot[1] = ps
+    tile = 32
+    inplane = lax.broadcasted_iota(jnp.int32, (1, plane), 1)
+    ys = (inplane // GRID).astype(F32)
+    zs = (inplane % GRID).astype(F32)
+    scale = 1.0 / math.sqrt(total_points)
+
+    def table_tile(i, carry):
+        rows = pl.ds(pl.multiple_of(i * tile, tile), tile)
+        rows_im = pl.ds(pl.multiple_of(width + i * tile, tile), tile)
+        g = gcol[rows, :]
+        qc, qs = unit(g[:, 1:2] * ys + g[:, 2:3] * zs)
+        qc = qc * scale
+        qs = qs * scale
+        pc = prot[0, rows, :]
+        ps = prot[1, rows, :]
+        for xx in range(GRID):
+            cp = pc[:, xx : xx + 1]
+            sp = ps[:, xx : xx + 1]
+            cols = slice((xx % xs_per) * plane, (xx % xs_per + 1) * plane)
+            table[xx // xs_per, rows, cols] = (cp * qc - sp * qs).astype(BF16)
+            table[xx // xs_per, rows_im, cols] = (sp * qc + cp * qs).astype(BF16)
+        return carry
+
+    lax.fori_loop(0, width // tile, table_tile, 0)
+
+    for t in range(1, nz):
+        slot = zpeer(t) * 2 + x
+        c = copy(cond_all.at[slot], cond_all.at[slot], ag_fwd.at[t], ag_recv.at[slot], xn, k)
+        c.wait_recv()
+        c.start()
+        sends.append(c)
+
+    def step(t, carry):
+        zz = zpeer(t)
+        near = zz * 2 + x
+        far = zz * 2 + 1 - x
+        copy(cond_all.at[far], cond_all.at[far], ag_send.at[0], ag_recv.at[far], xn, k).wait_recv()
+        for h in range(2):
+            conds = cond_all[zz * 2 + h].astype(F32)
+            start = pl.multiple_of((zz * 2 + h) * block_points, block_points)
+            vals = val_ref[:, pl.ds(start, block_points)].astype(F32)
+            for v in range(n_val):
+                pair[v * n_cond : (v + 1) * n_cond, h * block_points : (h + 1) * block_points] = (
+                    conds * vals[v : v + 1, :]
+                ).astype(BF16)
+
+        def rows_of(i, c):
+            rows = pl.ds(pl.multiple_of(i * 256, 256), 256)
+            part = lax.dot_general(table[zz, rows, :], pair[...], NT, preferred_element_type=F32)
+
+            @pl.when(t == 0)
+            def _():
+                acc[rows, :] = part
+
+            @pl.when(t > 0)
+            def _():
+                acc[rows, :] += part
+
+            return c
+
+        lax.fori_loop(0, 2 * width // 256, rows_of, 0)
+        return carry
+
+    lax.fori_loop(0, nz, step, 0)
+
+    n_pair = n_val * n_cond
+    pos = lax.broadcasted_iota(jnp.int32, (1, n_pair), 1)
+    ve_row = jnp.zeros((1, n_pair), F32)
+    for v in range(n_val):
+        ve_row = jnp.where(pos // n_cond == v, ve_ref[v], ve_row)
+    ce_row = jnp.zeros((1, n_pair), F32)
+    for c in range(n_cond):
+        ce_row = jnp.where(pos % n_cond == c, ce_ref[c], ce_row)
+    norm = 1.0 / math.sqrt(n_val * n_band * n_cond * n_blk)
+    factor = -1.0 / (ce_row - ve_row) * norm
+
+    ctile = 64
+
+    def weigh(i, carry):
+        rows = pl.ds(pl.multiple_of(i * ctile, ctile), ctile)
+        rows_im = pl.ds(pl.multiple_of(width + i * ctile, ctile), ctile)
+        a = acc[rows, :].astype(BF16).astype(F32)
+        bb = acc[rows_im, :].astype(BF16).astype(F32)
+        wgt[rows, 0:n_pair] = (a * factor).astype(BF16)
+        wgt[rows, n_pair : 2 * n_pair] = (bb * factor).astype(BF16)
+        dst_[rows, 0:n_pair] = (a - bb).astype(BF16)
+        dst_[rows, n_pair : 2 * n_pair] = (a + bb).astype(BF16)
+        return carry
+
+    lax.fori_loop(0, width // ctile, weigh, 0)
+
+    def half(blk):
+        cols = pl.ds(pl.multiple_of(blk * col_block, col_block), col_block)
+        return lax.dot_general(wgt[...], dst_[cols, :], NT, preferred_element_type=F32)
+
+    theirs = half(kn)
+    for i in range(n_band):
+        send1[i % 2, i // 2] = theirs[i * row_block : (i + 1) * row_block, :].astype(BF16)
+    first = copy(send1.at[1 - x], recv1.at[1 - x], s1_send.at[0], s1_recv.at[0], b, kn)
+    second = copy(send1.at[x], recv1.at[x], s1_send.at[1], s1_recv.at[1], b, kn)
+    first.start()
+    second.start()
+    mine = half(k)
+    for i in range(n_band):
+        own1[i % 2, i // 2] = mine[i * row_block : (i + 1) * row_block, :]
+
+    first.wait_recv()
+    xcopies = []
+    for t in list(range(1, nz)) + [0]:
+        zz = zpeer(t)
+        sendx[zz] = (own1[1 - x, zz] + recv1[1 - x, zz].astype(F32)).astype(BF16)
+        c = copy(sendx.at[zz], recvx.at[zz], sx_send.at[zz], sx_recv.at[zz], xn, k)
+        c.start()
+        xcopies.append(c)
+    second.wait_recv()
+
+    zcopies = []
+    for i, t in enumerate(list(range(1, nz)) + [0]):
+        zz = zpeer(t)
+        xcopies[i].wait_recv()
+        total = own1[x, zz] + recv1[x, zz].astype(F32) + recvx[zz].astype(F32)
+        if t == 0:
+            final = total
+        else:
+            sendz[zz] = total.astype(BF16)
+            c = copy(sendz.at[zz], recvz.at[z], sz_send.at[zz], sz_recv.at[z], zz * 2 + x, k)
+            c.start()
+            zcopies.append(c)
+    for t in range(1, nz):
+        zz = zpeer(t)
+        copy(sendz.at[zz], recvz.at[zz], sz_send.at[zz], sz_recv.at[zz], zz * 2 + x, k).wait_recv()
+        final = final + recvz[zz].astype(F32)
+
+    packed_rows = row_block // 2
+    place = lax.rem(b, per_blk)
+    for j in range(per_blk):
+        block = final[:, j * row_block : (j + 1) * row_block]
+        sende[j] = jnp.concatenate([block[:packed_rows], block[packed_rows:]], axis=1).astype(BF16)
+
+        @pl.when(k * per_blk + j != b)
+        def _():
+            copy(sende.at[j], recve.at[place], se_send.at[j], se_recv.at[place], k * per_blk + j, mirror_blk).start()
+
+        @pl.when(k * per_blk + j == b)
+        def _():
+            other[j * row_block : (j + 1) * row_block, :] = block
+
+    for j in range(per_blk):
+        @pl.when(k * per_blk + j != b)
+        def _():
+            copy(sende.at[j], recve.at[j], se_send.at[j], se_recv.at[j], k * per_blk + j, mirror_blk).wait_recv()
+            got = recve[j].astype(F32)
+            other[j * row_block : j * row_block + packed_rows, :] = got[:, :row_block]
+            other[j * row_block + packed_rows : (j + 1) * row_block, :] = got[:, row_block:]
+
+    mirror = jnp.transpose(other[...])
+    out_ref[0] = (final + mirror) * 0.5
+    out_ref[1] = (final - mirror) * 0.5
+
+    for c in sends + xcopies + zcopies + [first, second]:
+        c.wait_send()
+    for j in range(per_blk):
+        @pl.when(k * per_blk + j != b)
+        def _():
+            copy(sende.at[j], recve.at[j], se_send.at[j], se_recv.at[j], k * per_blk + j, mirror_blk).wait_send()
+
+
+def fused(valence, conduction, val_energy, cond_energy, gvectors):
+    n_band = lax.axis_size("band")
+    n_blk = lax.axis_size("blk")
+    nz = n_band // 2
+    n_val, total_points = valence.shape
+    block_points, n_cond = conduction.shape
+    width = gvectors.shape[1]
+    row_block = width // n_band
+    col_block = width // n_blk
+    per_blk = col_block // row_block
+    n_pair = n_val * n_cond
+    dma = pltpu.SemaphoreType.DMA
+    vmem = pl.BlockSpec(memory_space=pltpu.VMEM)
+    smem = pl.BlockSpec(memory_space=pltpu.SMEM)
+    return pl.pallas_call(
+        functools.partial(chi_kernel, n_band, n_blk),
+        out_shape=jax.ShapeDtypeStruct((2, row_block, col_block), F32),
+        in_specs=[vmem, vmem, smem, smem, vmem],
+        out_specs=vmem,
+        scratch_shapes=[
+            pltpu.VMEM((8, width), F32),
+            pltpu.VMEM((width, 8), F32),
+            pltpu.VMEM((2, width, 128), F32),
+            pltpu.VMEM((n_band, n_cond, block_points), BF16),
+            pltpu.VMEM((nz, 2 * width, 2 * block_points), BF16),
+            pltpu.VMEM((n_pair, 2 * block_points), BF16),
+            pltpu.VMEM((2 * width, n_pair), F32),
+            pltpu.VMEM((width, 2 * n_pair), BF16),
+            pltpu.VMEM((width, 2 * n_pair), BF16),
+            pltpu.VMEM((2, nz, row_block, col_block), BF16),
+            pltpu.VMEM((2, nz, row_block, col_block), F32),
+            pltpu.VMEM((2, nz, row_block, col_block), BF16),
+            pltpu.VMEM((nz, row_block, col_block), BF16),
+            pltpu.VMEM((nz, row_block, col_block), BF16),
+            pltpu.VMEM((nz, row_block, col_block), BF16),
+            pltpu.VMEM((nz, row_block, col_block), BF16),
+            pltpu.VMEM((per_blk, row_block // 2, 2 * row_block), BF16),
+            pltpu.VMEM((per_blk, row_block // 2, 2 * row_block), BF16),
+            pltpu.VMEM((col_block, row_block), F32),
+            dma((nz,)), dma((nz,)), dma((n_band,)), dma((2,)), dma((2,)),
+            dma((nz,)), dma((nz,)), dma((nz,)), dma((nz,)), dma((per_blk,)), dma((per_blk,)),
+        ],
+        compiler_params=pltpu.CompilerParams(
+            collective_id=0, has_side_effects=True, vmem_limit_bytes=48 * 2**20
+        ),
+    )(valence, conduction, val_energy, cond_energy, gvectors)
 
 
 def table_rows(gvectors, grid, start, count):
@@ -76,6 +388,17 @@
     return lax.dynamic_slice_in_dim(mine, blk_index * col_block, col_block, 2)
 
 
+def fits(mesh, valence, conduction, gvectors):
+    n_band, n_blk, parts = mesh.shape["band"], mesh.shape["blk"], mesh.shape["groups"]
+    width = gvectors.shape[1] // parts
+    return (
+        n_blk == 2 and n_band % 2 == 0 and n_band <= 16 and n_band % n_blk == 0
+        and width // n_band == 64 and valence.shape[1] == GRID**3
+        and conduction.shape[0] // n_band % (GRID * GRID) == 0
+        and conduction.shape[1] // (parts * n_blk) % 16 == 0
+    )
+
+
 def solution(mesh):
     in_specs = (
         P(("groups", "band"), None),
@@ -85,6 +408,11 @@
         P(None, "groups"),
     )
     out_specs = P(None, ("groups", "band"), "blk")
-    return jax.shard_map(
-        per_device, mesh=mesh, in_specs=in_specs, out_specs=out_specs, check_vma=False
-    )
+
+    def run(valence, conduction, val_energy, cond_energy, gvectors):
+        body = fused if fits(mesh, valence, conduction, gvectors) else per_device
+        return jax.shard_map(
+            body, mesh=mesh, in_specs=in_specs, out_specs=out_specs, check_vma=False
+        )(valence, conduction, val_energy, cond_energy, gvectors)
+
+    return run

time: 195 us -> 37.8 us (0.19)
  waiting for transfers between devices: 104 us -> 0 us
  other arithmetic: 39.4 us -> 0 us
  Pallas kernels: 0 us -> 36 us
  blocking collectives: 26.1 us -> 0 us
  between operations: 13.6 us -> 0.06 us
  matrix products: 7.99 us -> 0 us
    psum x1 -> x0, waiting for transfers between devices: 104 us -> none  [per_device(): total = lax.psum(jnp.stack([real_part, imag_part]), ('band', 'blk'))]
    another operation x3 -> x0, other arithmetic: 38.2 us -> none
    pallas_call x0 -> x1, Pallas kernels: none -> 36 us  [fused(): pl.pallas_call(functools.partial(chi_kernel, n_band, n_blk), out_shape=ja...]
    all_gather x1 -> x0, blocking collectives: 26.1 us -> none  [per_device(): gathered = lax.all_gather(conduction, 'band', axis=0, tiled=True)]
    dot_general x12 -> x0, matrix products: 7.99 us -> none  [the longest x8 6.11 us: per_device(): jnp.dot(pair, tab_block, preferred_element_type=jnp.float32)]
  transfers between devices with their start and end apart: 1 -> 0, of which waited for: 1 -> 0; matrix products, arithmetic and copies ran while one was open for 0% -> 0% of each run, Pallas kernels for 0% -> 0%
where the time goes in v1:
time: 37.8 us; the launch traced here: 37.6 us
  Pallas kernels  36 us (95%)
  local copies, waits for them, and re-layouts  1.6 us (4%)
    pallas_call x1, Pallas kernels, fused(): pl.pallas_call(functools.partial(chi_kernel, n_band, n_blk), out_shape=ja...  36 us
    unnamed x10, local copies, waits for them, and re-layouts  1.6 us

profile of v1, /device:TPU:1, one launch (start us, length us, event | category | flops | bytes accessed | tf_op | source)
XLA Modules:
  0.0 37.6 jit_solution(8508138489759801262)
XLA Ops:
  0.0 0.0 copy-start.1
  0.0 0.0 copy-start.3
  0.0 0.0 copy-start.2
  0.0 0.0 copy-start
  0.0 0.9 %copy.6.cond_ref = bf16[512,32]{1,0:T(8,128)(2,1)S(1)} copy(bf16[512,32]{0,1:T(8,128)(2,1)} %param.6) | data formatting | bytes 65536 | tf_op args[1]
  1.0 0.0 copy-done.1
  1.0 0.0 copy-done.3
  1.0 0.0 copy-done.2
  1.0 0.0 copy-done
  1.0 36.0 %shard_map.55 = f32[2,64,256]{2,1,0:T(8,128)S(1)} custom-call(bf16[16,4096]{1,0:T(8,128)(2,1)S(1)} %copy-done, bf16[512,32]{1,0:T(8,128)(2,1)S(1)} %copy.6.cond_ref, f32[16]{0:T(128)S(1)} %copy-done.2, f32[32]{0:T(128)S(1)} %copy-done.3, s32[3,512]{1,0:T(4,128)S(1)} %copy-done.1), custom_call_target="tpu_custom_call" | custom-call | tf_op jit(solution)/shard_map/pallas_call | solution.py:289
  37.0 0.7 %copy.8 = f32[2,64,256]{2,1,0:T(8,128)} copy(f32[2,64,256]{2,1,0:T(8,128)S(1)} %shard_map.55) | data formatting | bytes 262144
Async XLA Ops:
  0.0 1.0 %copy-start.1 = (s32[3,512]{1,0:T(4,128)S(1)}, s32[3,512]{1,0:T(4,128)}, u32[]{:S(2)}) copy-start(s32[3,512]{1,0:T(4,128)} %gv_ref.1) | copy-start | bytes 18436
  0.0 1.0 %copy-start.3 = (f32[32]{0:T(128)S(1)}, f32[32]{0:T(128)}, u32[]{:S(2)}) copy-start(f32[32]{0:T(128)} %ce_ref.1) | copy-start | bytes 388
  0.0 1.0 %copy-start.2 = (f32[16]{0:T(128)S(1)}, f32[16]{0:T(128)}, u32[]{:S(2)}) copy-start(f32[16]{0:T(128)} %ve_ref.1) | copy-start | bytes 196
  0.0 1.0 %copy-start = (bf16[16,4096]{1,0:T(8,128)(2,1)S(1)}, bf16[16,4096]{1,0:T(8,128)(2,1)}, u32[]{:S(2)}) copy-start(bf16[16,4096]{1,0:T(8,128)(2,1)} %val_ref.1) | copy-start | bytes 393220

commit v2 on v1

--- a/solution.py
+++ b/solution.py
@@ -32,18 +32,18 @@
 
 
 def chi_kernel(
-    n_band, n_blk, val_ref, cond_ref, ve_ref, ce_ref, gv_ref, out_ref,
+    n_band, n_blk, val_hbm, cond_hbm, ve_hbm, ce_hbm, gv_hbm, out_ref,
+    val_ref, ve_ref, ce_ref, gv_ref,
     gpad, gcol, prot, cond_all, table, pair, acc, wgt, dst_,
     send1, own1, recv1, sendx, recvx, sendz, recvz, sende, recve, other,
-    ag_send, ag_fwd, ag_recv, s1_send, s1_recv, sx_send, sx_recv, sz_send, sz_recv, se_send, se_recv,
+    in_sem, ag_send, ag_fwd, ag_recv, s1_send, s1_recv, sx_send, sx_recv, sz_send, sz_recv, se_send, se_recv,
 ):
     nz = n_band // 2
-    n_val, total_points = val_ref.shape
-    block_points, n_cond = cond_ref.shape
-    width = gv_ref.shape[1]
-    zpoints = 2 * block_points
+    n_val, total_points = val_hbm.shape
+    n_cond, block_points = cond_hbm.shape
+    width = gv_hbm.shape[1]
     plane = GRID * GRID
-    xs_per = zpoints // plane
+    xs_per = block_points // plane
     row_block = width // n_band
     col_block = width // n_blk
     per_blk = col_block // row_block
@@ -82,21 +82,29 @@
         def _():
             greet(k * per_blk + j, mirror_blk)
 
-    eye = (
-        lax.broadcasted_iota(jnp.int32, (n_cond, n_cond), 0) == lax.broadcasted_iota(jnp.int32, (n_cond, n_cond), 1)
-    ).astype(F32).astype(BF16)
-    cond_all[b] = lax.dot_general(eye, cond_ref[...], NT, preferred_element_type=F32).astype(BF16)
+    cond_ref = cond_all.at[b]
+    loads = [
+        pltpu.make_async_copy(src, dst, in_sem.at[i])
+        for i, (src, dst) in enumerate(
+            [(gv_hbm, gv_ref), (cond_hbm, cond_ref), (val_hbm, val_ref), (ve_hbm, ve_ref), (ce_hbm, ce_ref)]
+        )
+    ]
+    for c in loads:
+        c.start()
+    loads[0].wait()
 
     pl.semaphore_wait(barrier, 1 + nz + per_blk - jnp.where(mirror_blk == k, 1, 0))
 
+    for c in loads[1:]:
+        c.wait()
     sends = []
+    c = copy(cond_ref, cond_all.at[b], ag_send.at[0], ag_recv.at[b], xn, k)
+    c.start()
+    sends.append(c)
     for t in range(1, nz):
-        c = copy(cond_all.at[b], cond_all.at[b], ag_send.at[t], ag_recv.at[b], zpeer(t) * 2 + x, k)
+        c = copy(cond_ref, cond_all.at[b], ag_send.at[t], ag_recv.at[b], zpeer(t) * 2 + x, k)
         c.start()
         sends.append(c)
-    c = copy(cond_all.at[b], cond_all.at[b], ag_send.at[0], ag_recv.at[b], xn, k)
-    c.start()
-    sends.append(c)
 
     gpad[...] = jnp.zeros_like(gpad)
     gpad[0:3, :] = gv_ref[...].astype(F32)
@@ -120,55 +128,62 @@
         qs = qs * scale
         pc = prot[0, rows, :]
         ps = prot[1, rows, :]
-        for xx in range(GRID):
+        flip = jnp.broadcast_to(pc[:, GRID // 2 : GRID // 2 + 1], (tile, plane)).astype(BF16)
+        for xx in range(GRID // 2):
             cp = pc[:, xx : xx + 1]
             sp = ps[:, xx : xx + 1]
-            cols = slice((xx % xs_per) * plane, (xx % xs_per + 1) * plane)
-            table[xx // xs_per, rows, cols] = (cp * qc - sp * qs).astype(BF16)
-            table[xx // xs_per, rows_im, cols] = (sp * qc + cp * qs).astype(BF16)
+            re = (cp * qc - sp * qs).astype(BF16)
+            im = (sp * qc + cp * qs).astype(BF16)
+            for at, r, m in ((xx, re, im), (xx + GRID // 2, re * flip, im * flip)):
+                cols = slice((at % xs_per) * plane, (at % xs_per + 1) * plane)
+                table[at // xs_per, rows, cols] = r
+                table[at // xs_per, rows_im, cols] = m
         return carry
 
     lax.fori_loop(0, width // tile, table_tile, 0)
 
+    def arrived(slot):
+        copy(cond_all.at[slot], cond_all.at[slot], ag_send.at[0], ag_recv.at[slot], xn, k).wait_recv()
+
+    def accumulate(blocks, first):
+        for i, (slot, conds) in enumerate(blocks):
+            conds = conds[...].astype(F32)
+            start = pl.multiple_of(slot * block_points, block_points)
+            vals = val_ref[:, pl.ds(start, block_points)].astype(F32)
+            for v in range(n_val):
+                pair[i, v * n_cond : (v + 1) * n_cond, :] = (conds * vals[v : v + 1, :]).astype(BF16)
+
+        def rows_of(r, carry):
+            rows = pl.ds(pl.multiple_of(r * dot_rows, dot_rows), dot_rows)
+            part = None
+            for i, (slot, _) in enumerate(blocks):
+                term = lax.dot_general(table[slot, rows, :], pair[i], NT, preferred_element_type=F32)
+                part = term if part is None else part + term
+            if first:
+                acc[rows, :] = part
+            else:
+                acc[rows, :] += part
+            return carry
+
+        lax.fori_loop(0, 2 * width // dot_rows, rows_of, 0)
+
+    dot_rows = 2 * width
+
+    near = []
+    far = []
     for t in range(1, nz):
         slot = zpeer(t) * 2 + x
+        arrived(slot)
         c = copy(cond_all.at[slot], cond_all.at[slot], ag_fwd.at[t], ag_recv.at[slot], xn, k)
-        c.wait_recv()
         c.start()
         sends.append(c)
-
-    def step(t, carry):
-        zz = zpeer(t)
-        near = zz * 2 + x
-        far = zz * 2 + 1 - x
-        copy(cond_all.at[far], cond_all.at[far], ag_send.at[0], ag_recv.at[far], xn, k).wait_recv()
-        for h in range(2):
-            conds = cond_all[zz * 2 + h].astype(F32)
-            start = pl.multiple_of((zz * 2 + h) * block_points, block_points)
-            vals = val_ref[:, pl.ds(start, block_points)].astype(F32)
-            for v in range(n_val):
-                pair[v * n_cond : (v + 1) * n_cond, h * block_points : (h + 1) * block_points] = (
-                    conds * vals[v : v + 1, :]
-                ).astype(BF16)
-
-        def rows_of(i, c):
-            rows = pl.ds(pl.multiple_of(i * 256, 256), 256)
-            part = lax.dot_general(table[zz, rows, :], pair[...], NT, preferred_element_type=F32)
-
-            @pl.when(t == 0)
-            def _():
-                acc[rows, :] = part
-
-            @pl.when(t > 0)
-            def _():
-                acc[rows, :] += part
-
-            return c
-
-        lax.fori_loop(0, 2 * width // 256, rows_of, 0)
-        return carry
-
-    lax.fori_loop(0, nz, step, 0)
+        near.append((slot, cond_all.at[slot]))
+        far.append((zpeer(t) * 2 + 1 - x, cond_all.at[zpeer(t) * 2 + 1 - x]))
+    arrived(xn)
+    accumulate([(b, cond_ref), (xn, cond_all.at[xn])] + near, True)
+    for slot, _ in far:
+        arrived(slot)
+    accumulate(far, False)
 
     n_pair = n_val * n_cond
     pos = lax.broadcasted_iota(jnp.int32, (1, n_pair), 1)
@@ -285,19 +300,22 @@
     n_pair = n_val * n_cond
     dma = pltpu.SemaphoreType.DMA
     vmem = pl.BlockSpec(memory_space=pltpu.VMEM)
-    smem = pl.BlockSpec(memory_space=pltpu.SMEM)
     return pl.pallas_call(
         functools.partial(chi_kernel, n_band, n_blk),
         out_shape=jax.ShapeDtypeStruct((2, row_block, col_block), F32),
-        in_specs=[vmem, vmem, smem, smem, vmem],
+        in_specs=[pl.BlockSpec(memory_space=pltpu.HBM)] * 5,
         out_specs=vmem,
         scratch_shapes=[
+            pltpu.VMEM(valence.shape, BF16),
+            pltpu.SMEM(val_energy.shape, F32),
+            pltpu.SMEM(cond_energy.shape, F32),
+            pltpu.VMEM(gvectors.shape, jnp.int32),
             pltpu.VMEM((8, width), F32),
             pltpu.VMEM((width, 8), F32),
             pltpu.VMEM((2, width, 128), F32),
             pltpu.VMEM((n_band, n_cond, block_points), BF16),
-            pltpu.VMEM((nz, 2 * width, 2 * block_points), BF16),
-            pltpu.VMEM((n_pair, 2 * block_points), BF16),
+            pltpu.VMEM((n_band, 2 * width, block_points), BF16),
+            pltpu.VMEM((nz + 1, n_pair, block_points), BF16),
             pltpu.VMEM((2 * width, n_pair), F32),
             pltpu.VMEM((width, 2 * n_pair), BF16),
             pltpu.VMEM((width, 2 * n_pair), BF16),
@@ -311,13 +329,13 @@
             pltpu.VMEM((per_blk, row_block // 2, 2 * row_block), BF16),
             pltpu.VMEM((per_blk, row_block // 2, 2 * row_block), BF16),
             pltpu.VMEM((col_block, row_block), F32),
-            dma((nz,)), dma((nz,)), dma((n_band,)), dma((2,)), dma((2,)),
+            dma((5,)), dma((nz,)), dma((nz,)), dma((n_band,)), dma((2,)), dma((2,)),
             dma((nz,)), dma((nz,)), dma((nz,)), dma((nz,)), dma((per_blk,)), dma((per_blk,)),
         ],
         compiler_params=pltpu.CompilerParams(
             collective_id=0, has_side_effects=True, vmem_limit_bytes=48 * 2**20
         ),
-    )(valence, conduction, val_energy, cond_energy, gvectors)
+    )(valence, conduction.T, val_energy, cond_energy, gvectors)
 
 
 def table_rows(gvectors, grid, start, count):

time: 37.8 us -> 34.4 us (0.910)
  Pallas kernels: 36 us -> 30.5 us
  local copies, waits for them, and re-layouts: 1.6 us -> 3.68 us
    pallas_call x1, Pallas kernels: 36 us -> 30.5 us  [fused(): pl.pallas_call(functools.partial(chi_kernel, n_band, n_blk), out_shape=ja...]
    unnamed x10 -> x11, local copies, waits for them, and re-layouts: 1.6 us -> 3.68 us
where the time goes in v2:
time: 34.4 us; the launch traced here: 34.2 us
  Pallas kernels  30.5 us (89%)
  local copies, waits for them, and re-layouts  3.68 us (11%)
    pallas_call x1, Pallas kernels, fused(): pl.pallas_call(functools.partial(chi_kernel, n_band, n_blk), out_shape=ja...  30.5 us
    unnamed x11, local copies, waits for them, and re-layouts  3.68 us

profile of v2, /device:TPU:1, one launch (start us, length us, event | category | flops | bytes accessed | tf_op | source)
XLA Modules:
  0.0 34.2 jit_solution(8762120203050901775)
XLA Ops:
  0.0 0.0 copy-start.4
  0.0 0.0 copy-start.3
  0.0 0.7 %copy-done.4 = f32[32]{0:T(128)S(1)} copy-done((f32[32]{0:T(128)S(1)}, f32[32]{0:T(128)}, u32[]{:S(2)}) %copy-start.4) | copy-done | bytes 152
  0.7 0.0 copy-done.3
  0.7 0.0 copy-start
  0.7 0.9 %copy-done = bf16[16,4096]{1,0:T(8,128)(2,1)S(1)} copy-done((bf16[16,4096]{1,0:T(8,128)(2,1)S(1)}, bf16[16,4096]{1,0:T(8,128)(2,1)}, u32[]{:S(2)}) %copy-start) | copy-done | bytes 131096
  1.6 0.0 copy-start.1
  1.6 0.8 %copy-done.1 = bf16[512,32]{0,1:T(8,128)(2,1)S(1)} copy-done((bf16[512,32]{0,1:T(8,128)(2,1)S(1)}, bf16[512,32]{0,1:T(8,128)(2,1)}, u32[]{:S(2)}) %copy-start.1) | copy-done | bytes 32792
  2.3 0.0 copy-start.2
  2.3 0.7 %copy-done.2 = s32[3,512]{1,0:T(4,128)S(1)} copy-done((s32[3,512]{1,0:T(4,128)S(1)}, s32[3,512]{1,0:T(4,128)}, u32[]{:S(2)}) %copy-start.2) | copy-done | bytes 6168
  3.0 30.5 %shard_map.55 = f32[2,64,256]{2,1,0:T(8,128)S(1)} custom-call(bf16[16,4096]{1,0:T(8,128)(2,1)S(1)} %copy-done, bf16[32,512]{1,0:T(8,128)(2,1)S(1)} %bitcast.1, f32[16]{0:T(128)S(1)} %copy-done.3, f32[32]{0:T(128)S(1)} %copy-done.4, s32[3,512]{1,0:T(4,128)S(1)} %copy-done.2), custom_call_target="tpu_custom_call" | custom-call | tf_op jit(solution)/shard_map/pallas_call | solution.py:303
  33.5 0.7 %copy.7 = f32[2,64,256]{2,1,0:T(8,128)} copy(f32[2,64,256]{2,1,0:T(8,128)S(1)} %shard_map.55) | data formatting | bytes 262144
Async XLA Ops:
  0.0 0.7 %copy-start.4 = (f32[32]{0:T(128)S(1)}, f32[32]{0:T(128)}, u32[]{:S(2)}) copy-start(f32[32]{0:T(128)} %ce_hbm.1) | copy-start | bytes 388
  0.0 0.7 %copy-start.3 = (f32[16]{0:T(128)S(1)}, f32[16]{0:T(128)}, u32[]{:S(2)}) copy-start(f32[16]{0:T(128)} %ve_hbm.1) | copy-start | bytes 196
  0.7 0.9 %copy-start = (bf16[16,4096]{1,0:T(8,128)(2,1)S(1)}, bf16[16,4096]{1,0:T(8,128)(2,1)}, u32[]{:S(2)}) copy-start(bf16[16,4096]{1,0:T(8,128)(2,1)} %val_hbm.1) | copy-start | bytes 393220
  1.6 0.8 %copy-start.1 = (bf16[512,32]{0,1:T(8,128)(2,1)S(1)}, bf16[512,32]{0,1:T(8,128)(2,1)}, u32[]{:S(2)}) copy-start(bf16[512,32]{0,1:T(8,128)(2,1)} %param.6) | copy-start | bytes 98308
  2.3 0.7 %copy-start.2 = (s32[3,512]{1,0:T(4,128)S(1)}, s32[3,512]{1,0:T(4,128)}, u32[]{:S(2)}) copy-start(s32[3,512]{1,0:T(4,128)} %gv_hbm.1) | copy-start | bytes 18436

commit v3 on v2

--- a/solution.py
+++ b/solution.py
@@ -92,19 +92,6 @@
     for c in loads:
         c.start()
     loads[0].wait()
-
-    pl.semaphore_wait(barrier, 1 + nz + per_blk - jnp.where(mirror_blk == k, 1, 0))
-
-    for c in loads[1:]:
-        c.wait()
-    sends = []
-    c = copy(cond_ref, cond_all.at[b], ag_send.at[0], ag_recv.at[b], xn, k)
-    c.start()
-    sends.append(c)
-    for t in range(1, nz):
-        c = copy(cond_ref, cond_all.at[b], ag_send.at[t], ag_recv.at[b], zpeer(t) * 2 + x, k)
-        c.start()
-        sends.append(c)
 
     gpad[...] = jnp.zeros_like(gpad)
     gpad[0:3, :] = gv_ref[...].astype(F32)
@@ -140,7 +127,21 @@
                 table[at // xs_per, rows_im, cols] = m
         return carry
 
-    lax.fori_loop(0, width // tile, table_tile, 0)
+    lax.fori_loop(0, width // tile // 2, table_tile, 0)
+    pl.semaphore_wait(barrier, 1 + nz + per_blk - jnp.where(mirror_blk == k, 1, 0))
+
+    for c in loads[1:]:
+        c.wait()
+    sends = []
+    c = copy(cond_ref, cond_all.at[b], ag_send.at[0], ag_recv.at[b], xn, k)
+    c.start()
+    sends.append(c)
+    for t in range(1, nz):
+        c = copy(cond_ref, cond_all.at[b], ag_send.at[t], ag_recv.at[b], zpeer(t) * 2 + x, k)
+        c.start()
+        sends.append(c)
+
+    lax.fori_loop(width // tile // 2, width // tile, table_tile, 0)
 
     def arrived(slot):
         copy(cond_all.at[slot], cond_all.at[slot], ag_send.at[0], ag_recv.at[slot], xn, k).wait_recv()
@@ -165,9 +166,12 @@
                 acc[rows, :] += part
             return carry
 
-        lax.fori_loop(0, 2 * width // dot_rows, rows_of, 0)
-
-    dot_rows = 2 * width
+        for r in range(2 * width // dot_rows):
+            rows_of(r, 0)
+
+    dot_rows = 512
+
+    accumulate([(b, cond_ref)], True)
 
     near = []
     far = []
@@ -180,7 +184,7 @@
         near.append((slot, cond_all.at[slot]))
         far.append((zpeer(t) * 2 + 1 - x, cond_all.at[zpeer(t) * 2 + 1 - x]))
     arrived(xn)
-    accumulate([(b, cond_ref), (xn, cond_all.at[xn])] + near, True)
+    accumulate([(xn, cond_all.at[xn])] + near, False)
     for slot, _ in far:
         arrived(slot)
     accumulate(far, False)
@@ -228,7 +232,8 @@
 
     first.wait_recv()
     xcopies = []
-    for t in list(range(1, nz)) + [0]:
+    order = sorted(range(1, nz), key=lambda t: -min(t, nz - t)) + [0]
+    for t in order:
         zz = zpeer(t)
         sendx[zz] = (own1[1 - x, zz] + recv1[1 - x, zz].astype(F32)).astype(BF16)
         c = copy(sendx.at[zz], recvx.at[zz], sx_send.at[zz], sx_recv.at[zz], xn, k)
@@ -237,7 +242,7 @@
     second.wait_recv()
 
     zcopies = []
-    for i, t in enumerate(list(range(1, nz)) + [0]):
+    for i, t in enumerate(order):
         zz = zpeer(t)
         xcopies[i].wait_recv()
         total = own1[x, zz] + recv1[x, zz].astype(F32) + recvx[zz].astype(F32)

time: 34.4 us -> 33.7 us (0.980)
  Pallas kernels: 30.5 us -> 29.7 us
    pallas_call x1, Pallas kernels: 30.5 us -> 29.7 us  [fused(): pl.pallas_call(functools.partial(chi_kernel, n_band, n_blk), out_shape=ja...]
where the time goes in v3:
time: 33.7 us; the launch traced here: 33.4 us
  Pallas kernels  29.7 us (88%)
  local copies, waits for them, and re-layouts  3.68 us (11%)
    pallas_call x1, Pallas kernels, fused(): pl.pallas_call(functools.partial(chi_kernel, n_band, n_blk), out_shape=ja...  29.7 us
    unnamed x11, local copies, waits for them, and re-layouts  3.68 us

profile of v3, /device:TPU:1, one launch (start us, length us, event | category | flops | bytes accessed | tf_op | source)
XLA Modules:
  0.0 33.4 jit_solution(7641018983936933223)
XLA Ops:
  0.0 0.0 copy-start.4
  0.0 0.0 copy-start.3
  0.0 0.7 %copy-done.4 = f32[32]{0:T(128)S(1)} copy-done((f32[32]{0:T(128)S(1)}, f32[32]{0:T(128)}, u32[]{:S(2)}) %copy-start.4) | copy-done | bytes 152
  0.7 0.0 copy-done.3
  0.7 0.0 copy-start
  0.7 0.9 %copy-done = bf16[16,4096]{1,0:T(8,128)(2,1)S(1)} copy-done((bf16[16,4096]{1,0:T(8,128)(2,1)S(1)}, bf16[16,4096]{1,0:T(8,128)(2,1)}, u32[]{:S(2)}) %copy-start) | copy-done | bytes 131096
  1.6 0.0 copy-start.1
  1.6 0.8 %copy-done.1 = bf16[512,32]{0,1:T(8,128)(2,1)S(1)} copy-done((bf16[512,32]{0,1:T(8,128)(2,1)S(1)}, bf16[512,32]{0,1:T(8,128)(2,1)}, u32[]{:S(2)}) %copy-start.1) | copy-done | bytes 32792
  2.3 0.0 copy-start.2
  2.3 0.7 %copy-done.2 = s32[3,512]{1,0:T(4,128)S(1)} copy-done((s32[3,512]{1,0:T(4,128)S(1)}, s32[3,512]{1,0:T(4,128)}, u32[]{:S(2)}) %copy-start.2) | copy-done | bytes 6168
  3.0 29.7 %shard_map.55 = f32[2,64,256]{2,1,0:T(8,128)S(1)} custom-call(bf16[16,4096]{1,0:T(8,128)(2,1)S(1)} %copy-done, bf16[32,512]{1,0:T(8,128)(2,1)S(1)} %bitcast.1, f32[16]{0:T(128)S(1)} %copy-done.3, f32[32]{0:T(128)S(1)} %copy-done.4, s32[3,512]{1,0:T(4,128)S(1)} %copy-done.2), custom_call_target="tpu_custom_call" | custom-call | tf_op jit(solution)/shard_map/pallas_call | solution.py:308
  32.8 0.7 %copy.7 = f32[2,64,256]{2,1,0:T(8,128)} copy(f32[2,64,256]{2,1,0:T(8,128)S(1)} %shard_map.55) | data formatting | bytes 262144
Async XLA Ops:
  0.0 0.7 %copy-start.4 = (f32[32]{0:T(128)S(1)}, f32[32]{0:T(128)}, u32[]{:S(2)}) copy-start(f32[32]{0:T(128)} %ce_hbm.1) | copy-start | bytes 388
  0.0 0.7 %copy-start.3 = (f32[16]{0:T(128)S(1)}, f32[16]{0:T(128)}, u32[]{:S(2)}) copy-start(f32[16]{0:T(128)} %ve_hbm.1) | copy-start | bytes 196
  0.7 0.9 %copy-start = (bf16[16,4096]{1,0:T(8,128)(2,1)S(1)}, bf16[16,4096]{1,0:T(8,128)(2,1)}, u32[]{:S(2)}) copy-start(bf16[16,4096]{1,0:T(8,128)(2,1)} %val_hbm.1) | copy-start | bytes 393220
  1.6 0.8 %copy-start.1 = (bf16[512,32]{0,1:T(8,128)(2,1)S(1)}, bf16[512,32]{0,1:T(8,128)(2,1)}, u32[]{:S(2)}) copy-start(bf16[512,32]{0,1:T(8,128)(2,1)} %param.6) | copy-start | bytes 98308
  2.3 0.7 %copy-start.2 = (s32[3,512]{1,0:T(4,128)S(1)}, s32[3,512]{1,0:T(4,128)}, u32[]{:S(2)}) copy-start(s32[3,512]{1,0:T(4,128)} %gv_hbm.1) | copy-start | bytes 18436
